TPU v7x, 512 devices: a whole 4x4x16 slice. The times are simulated.
512 devices in a mesh: dp: 16 (over z), expert: 32 (over y, x, core).
Axes of the slice: x: 4, y: 4, z: 16, core: 2. Of those that a mesh axis runs over, the one named last changes fastest.
Arguments:
- tokens: bfloat16 [65536, 1024], P(('dp', 'expert')), may hold values from -6 to 6
- grad_out: bfloat16 [65536, 1024], P(('dp', 'expert')), may hold values from -6 to 6
- expert_ids: int32 [65536, 2], P(('dp', 'expert')), may hold values from 0 to 31, all different within a row; in each aligned block of 128 rows (0 to 127, 128 to 255, ...) at most 16 rows name the same one
- route_probs: bfloat16 [65536, 2], P(('dp', 'expert')), may hold values from 0.19921875 to 1
- gate_up_weight: bfloat16 [1024, 32, 1536], P('dp', 'expert'), may hold values from -0.1875 to 0.1875
- down_weight: bfloat16 [32, 768, 1024], P('expert'), may hold values from -0.21875 to 0.21875
- gate_up_scale_index: int32 [8, 32, 2], P(None, 'expert'), may hold values from 0 to 15
- down_scale_index: int32 [32, 6], P('expert'), may hold values from 0 to 15
- scale_table: float32 [16], replicated, may hold values from 0.5 to 2
Outputs:
- token_grad: bfloat16 [65536, 1024], P(('dp', 'expert'))
- prob_grad: float32 [65536, 2], P(('dp', 'expert'))
- gate_up_grad: bfloat16 [1024, 32, 1536], P('dp', 'expert')
- down_grad: bfloat16 [32, 768, 1024], P('expert')
Inputs may be any that keep to these rules, and one draw needn't show every extreme that they name: `expert_ids`: each row names two different experts. The 128 rows of one device name one expert at most 16 times, and in every draw some device's rows name some expert exactly 16 times.
All inputs are finite; a program needn't handle non-finite values.
Results may differ from a plain program's by a relative error of at most 0.022.
Values may be sent and summed in bfloat16 or wider, within the bound.
No kernel may reach another device: no remote copies, remote signals or barrier semaphores. Data moves between devices by JAX's collectives and lax.ppermute only.
A program may use at most 64 MiB of HBM per device.

v0:
```python
import jax
import jax.numpy as jnp
from jax import lax
from jax.sharding import PartitionSpec as P

QBLOCK = 128


def lookup(level_index, level_table):
    onehot = (level_index[..., None] == jnp.arange(level_table.shape[0], dtype=jnp.int32)).astype(
        level_table.dtype
    )
    return jnp.sum(onehot * level_table, axis=-1)


def slot_tables(routes, experts, capacity):
    flat_routes = routes.reshape(-1)
    expert_hits = (flat_routes[:, None] == jnp.arange(experts, dtype=jnp.int32)[None, :]).astype(
        jnp.int32
    )
    place = jnp.arange(flat_routes.shape[0], dtype=jnp.int32)
    earlier = (place[None, :] < place[:, None]).astype(jnp.bfloat16)
    before = jnp.dot(
        earlier, expert_hits.astype(jnp.bfloat16), preferred_element_type=jnp.float32
    ).astype(jnp.int32)
    slot_rank = jnp.sum(before * expert_hits, axis=1)
    destination = flat_routes * capacity + slot_rank
    table_hits = destination[:, None] == jnp.arange(experts * capacity, dtype=jnp.int32)[None, :]
    return table_hits.astype(jnp.float32).reshape(routes.shape[0], 2, experts * capacity)


def body(
    tokens,
    grad_out,
    expert_ids,
    route_probs,
    gate_up_weight,
    down_weight,
    gate_up_scale_index,
    down_scale_index,
    scale_table,
):
    high = lax.Precision.HIGHEST
    f32 = jnp.float32
    groups = lax.axis_size("expert")
    tok_dev = tokens.shape[0]
    model_width = tokens.shape[1]
    per_device = down_weight.shape[0]
    hidden = down_weight.shape[1]
    experts = per_device * groups
    capacity = 4 * tok_dev // experts
    slots_all = experts * capacity
    slot_hits = slot_tables(expert_ids, experts, capacity)
    either = (slot_hits[:, 0] + slot_hits[:, 1]).astype(jnp.bfloat16)
    row_shape = (groups, per_device, capacity, model_width)
    send_tokens = (
        jnp.einsum("ts,td->sd", either, tokens, preferred_element_type=f32)
        .astype(jnp.bfloat16)
        .reshape(row_shape)
    )
    send_grads = (
        jnp.einsum("ts,td->sd", either, grad_out, preferred_element_type=f32)
        .astype(jnp.bfloat16)
        .reshape(row_shape)
    )
    send_probs = (
        jnp.einsum("tks,tk->s", slot_hits, route_probs.astype(f32), precision=high)
        .astype(jnp.bfloat16)
        .reshape(row_shape[:3])
    )
    recv_tokens, recv_grads, recv_probs = (
        lax.all_to_all(send_tokens, "expert", split_axis=0, concat_axis=0, tiled=True),
        lax.all_to_all(send_grads, "expert", split_axis=0, concat_axis=0, tiled=True),
        lax.all_to_all(send_probs, "expert", split_axis=0, concat_axis=0, tiled=True),
    )
    level_rows = jnp.repeat(lookup(gate_up_scale_index, scale_table), QBLOCK, axis=0)
    full_scale = jnp.repeat(level_rows, hidden, axis=2)
    down_scale = jnp.repeat(lookup(down_scale_index, scale_table), QBLOCK, axis=1)
    down_eff = (down_weight.astype(f32) * down_scale[:, :, None]).astype(jnp.bfloat16)
    gathered = lax.all_gather(gate_up_weight, "dp", axis=0, tiled=True)
    gate_up_eff = (gathered.astype(f32) * full_scale).astype(jnp.bfloat16)
    projected = jnp.einsum("sjcd,djf->sjcf", recv_tokens, gate_up_eff, preferred_element_type=f32)
    gate_part = projected[..., :hidden]
    up_part = projected[..., hidden:]
    sigmoid_gate = jax.nn.sigmoid(gate_part)
    activated = gate_part * sigmoid_gate
    hidden_rows = (activated * up_part).astype(jnp.bfloat16)
    hidden_grad = jnp.einsum("sjcd,jfd->sjcf", recv_grads, down_eff, preferred_element_type=f32)
    probs_wide = recv_probs.astype(f32)[..., None]
    scaled_grad = probs_wide * hidden_grad
    gate_grad = scaled_grad * up_part * sigmoid_gate * (1.0 + gate_part * (1.0 - sigmoid_gate))
    up_grad = scaled_grad * activated
    joint_grad = jnp.concatenate([gate_grad, up_grad], axis=-1).astype(jnp.bfloat16)
    row_grads = jnp.einsum(
        "sjcf,djf->sjcd", joint_grad, gate_up_eff, preferred_element_type=f32
    ).astype(jnp.bfloat16)
    back_rows = lax.all_to_all(row_grads, "expert", split_axis=0, concat_axis=0, tiled=True)
    token_grad = jnp.dot(
        either, back_rows.reshape(slots_all, model_width), preferred_element_type=f32
    ).astype(jnp.bfloat16)
    expert_out = jnp.einsum("sjcf,jfd->sjcd", hidden_rows, down_eff, preferred_element_type=f32)
    back_out = lax.all_to_all(
        expert_out.astype(jnp.bfloat16), "expert", split_axis=0, concat_axis=0, tiled=True
    ).astype(expert_out.dtype)
    picked = jnp.einsum(
        "tks,sd->tkd", slot_hits, back_out.reshape(slots_all, model_width), precision=high
    )
    prob_grad = jnp.sum(picked * grad_out.astype(f32)[:, None, :], axis=-1)
    weighted = (probs_wide * hidden_rows.astype(f32)).astype(jnp.bfloat16)
    partial_sum = jnp.einsum("sjcd,sjcf->djf", recv_tokens, joint_grad, preferred_element_type=f32)
    gate_up_grad = lax.psum_scatter(
        (partial_sum * full_scale).astype(jnp.bfloat16), "dp", scatter_dimension=0, tiled=True
    )
    down_part = (
        jnp.einsum("sjcf,sjcd->jfd", weighted, recv_grads, preferred_element_type=f32)
        * down_scale[:, :, None]
    )
    down_grad = lax.psum(down_part.astype(jnp.bfloat16), "dp")
    return (token_grad, prob_grad, gate_up_grad, down_grad)


def solution(mesh):
    in_specs = (
        P(("dp", "expert"), None),
        P(("dp", "expert"), None),
        P(("dp", "expert"), None),
        P(("dp", "expert"), None),
        P("dp", "expert", None),
        P("expert", None, None),
        P(None, "expert", None),
        P("expert", None),
        P(),
    )
    out_specs = (
        P(("dp", "expert"), None),
        P(("dp", "expert"), None),
        P("dp", "expert", None),
        P("expert", None, None),
    )
    return jax.shard_map(body, mesh=mesh, in_specs=in_specs, out_specs=out_specs, check_vma=False)
```

profile of v0, /device:TPU:2, one launch (start us, length us, event | category | flops | bytes accessed | tf_op | source)
XLA Modules:
  0.0 353.9 jit_solution(2334480392853353179)
XLA Ops:
  7.2 0.0 copy-start
  7.2 0.0 all-gather.2.cloned.1.call-start
  7.2 0.7 all-gather.2.cloned.1.call-update
  7.9 0.8 copy.74
  8.7 0.1 eq.95
  8.8 0.2 fusion.16
  9.1 0.1 reduce_sum.39
  9.2 0.1 copy.75
  9.3 0.7 multiply_add_fusion
  10.0 0.9 fusion.34
  10.9 0.7 reshape.246
  11.6 9.4 %all-to-all-start = ((bf16[32,1,16]{2,1,0:T(2,128)(2,1)}), bf16[32,1,16]{2,1,0:T(2,128)(2,1)S(1)}, u32[]{:S(2)}, u32[]{:S(2)}) async-start(bf16[32,1,16]{2,1,0:T(2,128)(2,1)} %reshape.246), calls=%async_computation | async-start | bytes 32768 | tf_op jit(solution)/shard_map/all_to_all | solution.py:74
  21.0 0.1 fusion.35
  21.1 0.0 copy-start.9
  21.1 0.0 copy-start.10
  21.1 0.0 copy-start.13
  21.2 0.0 copy-start.4
  21.2 1.4 convolution_convert_fusion.1
  22.6 4.5 %all-to-all-done = bf16[32,1,16]{2,1,0:T(2,128)(2,1)S(1)} async-done(((bf16[32,1,16]{2,1,0:T(2,128)(2,1)}), bf16[32,1,16]{2,1,0:T(2,128)(2,1)S(1)}, u32[]{:S(2)}, u32[]{:S(2)}) %all-to-all-start) | async-done | bytes 1056 | tf_op jit(solution)/shard_map/all_to_all | solution.py:74
  27.2 5.7 %all-to-all-start.2 = ((bf16[32,1,16,1024]{3,2,1,0:T(8,128)(2,1)}), bf16[32,1,16,1024]{3,2,1,0:T(8,128)(2,1)}, u32[]{:S(2)}, u32[]{:S(2)}) async-start(bf16[32,1,16,1024]{3,2,1,0:T(8,128)(2,1)} %bitcast.19), calls=%async_computation.2 | async-start | bytes 2097152 | tf_op jit(solution)/shard_map/all_to_all | solution.py:72
  32.9 0.2 select_reduce_fusion
  33.0 0.1 broadcast_bitcast_fusion
  33.1 0.2 fusion.43
  33.3 0.7 broadcast_bitcast_fusion.1
  34.0 1.5 convolution_convert_fusion.2
  35.5 0.1 copy.78
  35.5 55.5 %all-gather.2.cloned.1.call-done = bf16[1024,1,1536]{2,0,1:T(8,128)(2,1)} async-done(((bf16[64,1,1536]{2,0,1:T(8,128)(2,1)}), bf16[1024,1,1536]{2,0,1:T(8,128)(2,1)}) %all-gather.2.cloned.1.call-update) | async-done | bytes 3145744 | tf_op jit(solution)/shard_map/all_gather | solution.py:80
  91.0 3.2 copy.76
  94.2 0.0 all-to-all-done.2
  94.2 7.2 %all-to-all-start.1 = ((bf16[32,1,16,1024]{3,2,1,0:T(8,128)(2,1)}), bf16[32,1,16,1024]{3,2,1,0:T(8,128)(2,1)}, u32[]{:S(2)}, u32[]{:S(2)}) async-start(bf16[32,1,16,1024]{3,2,1,0:T(8,128)(2,1)} %bitcast.139), calls=%async_computation.1 | async-start | bytes 2097152 | tf_op jit(solution)/shard_map/all_to_all | solution.py:73
  101.5 0.2 reduce-scatter.4.cloned.1.call-start
  101.7 0.8 broadcast_in_dim.14
  102.5 1.2 fusion.3
  103.7 1.7 copy-done.1
  105.4 1.7 copy-done.2
  107.1 5.1 %convolution_bitcast_fusion = f32[32,1,16,1536]{3,0,2,1:T(8,128)} fusion(bf16[1024,1536,1]{0,1,2:T(8,128)(2,1)S(1)} %fusion.3, bf16[32,1,16,1024]{3,2,1,0:T(8,128)(2,1)} %all-to-all-done.2), kind=kOutput, calls=%fused_computation.4 | convolution fusion | flops 1610612736 | bytes 7340032 | tf_op jit(solution)/shard_map/sjcd,djf->sjcf/dot_general | solution.py:82
  112.2 5.5 %all-to-all-done.1 = bf16[32,1,16,1024]{3,2,1,0:T(8,128)(2,1)} async-done(((bf16[32,1,16,1024]{3,2,1,0:T(8,128)(2,1)}), bf16[32,1,16,1024]{3,2,1,0:T(8,128)(2,1)}, u32[]{:S(2)}, u32[]{:S(2)}) %all-to-all-start.1) | async-done | bytes 1048608 | tf_op jit(solution)/shard_map/all_to_all | solution.py:73
  117.6 5.3 %fusion.31 = (bf16[32,16,768]{2,0,1:T(8,128)(2,1)S(1)}, bf16[32,16,768]{2,0,1:T(8,128)(2,1)S(1)}, bf16[32,1,16,768]{3,0,2,1:T(8,128)(2,1)}) fusion(f32[32,1,16,1536]{3,0,2,1:T(8,128)} %convolution_bitcast_fusion, bf16[32,1,16,1024]{3,2,1,0:T(8,128)(2,1)} %all-to-all-done.1, bf16[1,768,1024]{2,1,0:T(8,128)(2,1)S(1)} %copy-done.11, f32[768]{0:T(1024)S(1)} %copy-done.8, ...), kind=kOutput, calls=%fused_computation.49 | convolution fusion | flops 813957120 | bytes 8131584 | tf_op jit(solution)/shard_map/sjcd,jfd->sjcf/dot_general | solution.py:88
  123.0 3.8 %fusion.17 = f32[1536,1024,1]{1,0,2:T(8,128)S(1)} fusion(bf16[32,16,768]{2,0,1:T(8,128)(2,1)S(1)} %get-tuple-element.25, bf16[32,16,768]{2,0,1:T(8,128)(2,1)S(1)} %get-tuple-element.24, bf16[32,1,16,1024]{3,2,1,0:T(8,128)(2,1)} %all-to-all-done.2), kind=kOutput, calls=%fused_computation.36 | convolution fusion | flops 1613758464 | bytes 8912896 | tf_op jit(solution)/shard_map/sjcd,sjcf->djf/dot_general | solution.py:110
  126.8 1.8 fusion.2
  128.6 3.0 copy.96
  131.6 0.0 reduce-scatter.4.cloned.1.call-update
  131.6 1.4 copy-done.12
  133.0 0.2 copy-done.14
  133.2 1.1 fusion.12
  134.3 1.6 copy.86
  135.8 5.7 %all-to-all-start.4 = ((bf16[32,1,16,1024]{3,2,1,0:T(8,128)(2,1)}), bf16[32,1,16,1024]{3,2,1,0:T(8,128)(2,1)}, u32[]{:S(2)}, u32[]{:S(2)}) async-start(bf16[32,1,16,1024]{3,2,1,0:T(8,128)(2,1)} %copy.86), calls=%async_computation.4 | async-start | bytes 2097152 | tf_op jit(solution)/shard_map/all_to_all | solution.py:102
  141.6 0.3 all-reduce.2.cloned.1.call-start
  141.8 4.1 %fusion.11 = bf16[1,768,1024]{2,1,0:T(8,128)(2,1)} fusion(f32[768]{0:T(1024)S(1)} %copy-done.8, bf16[32,1,16,1024]{3,2,1,0:T(8,128)(2,1)} %all-to-all-done.1, bf16[32,1,16,768]{3,0,2,1:T(8,128)(2,1)} %get-tuple-element.26, f32[32,16]{0,1:T(8,128)S(1)} %copy.78), kind=kOutput, calls=%fused_computation.23 | convolution fusion | flops 808058880 | bytes 3412992 | tf_op jit(solution)/shard_map/sjcf,sjcd->jfd/dot_general | solution.py:115
  145.9 0.0 all-reduce.2.cloned.1.call-update
  146.0 3.2 fusion.13
  149.1 0.0 copy-start.5
  149.1 0.0 copy-start.7
  149.2 1.6 copy.85
  150.7 7.1 %all-to-all-done.4 = bf16[32,1,16,1024]{3,2,1,0:T(8,128)(2,1)} async-done(((bf16[32,1,16,1024]{3,2,1,0:T(8,128)(2,1)}), bf16[32,1,16,1024]{3,2,1,0:T(8,128)(2,1)}, u32[]{:S(2)}, u32[]{:S(2)}) %all-to-all-start.4) | async-done | bytes 1048608 | tf_op jit(solution)/shard_map/all_to_all | solution.py:102
  157.8 5.0 %all-to-all-start.3 = ((bf16[32,1,16,1024]{3,2,1,0:T(8,128)(2,1)}), bf16[32,1,16,1024]{3,2,1,0:T(8,128)(2,1)S(1)}, u32[]{:S(2)}, u32[]{:S(2)}) async-start(bf16[32,1,16,1024]{3,2,1,0:T(8,128)(2,1)} %copy.85), calls=%async_computation.3 | async-start | bytes 2097152 | tf_op jit(solution)/shard_map/all_to_all | solution.py:97
  162.9 2.4 fusion.14
  165.3 13.8 %all-to-all-done.3 = bf16[32,1,16,1024]{3,2,1,0:T(8,128)(2,1)S(1)} async-done(((bf16[32,1,16,1024]{3,2,1,0:T(8,128)(2,1)}), bf16[32,1,16,1024]{3,2,1,0:T(8,128)(2,1)S(1)}, u32[]{:S(2)}, u32[]{:S(2)}) %all-to-all-start.3) | async-done | bytes 1048608 | tf_op jit(solution)/shard_map/all_to_all | solution.py:97
  179.1 1.0 convolution_convert_fusion.4
  180.1 22.4 %reduce-scatter.4.cloned.1.call-done = bf16[64,1536]{1,0:T(8,128)(2,1)} async-done(((bf16[1024,1536]{1,0:T(8,128)(2,1)}), bf16[64,1536]{1,0:T(8,128)(2,1)}) %reduce-scatter.4.cloned.1.call-update) | async-done | bytes 196624
  202.5 1.1 copy.97
  203.6 0.8 copy.88
  204.5 140.2 %all-reduce.2.cloned.1.call-done = bf16[1,768,1024]{2,1,0:T(8,128)(2,1)} async-done(((bf16[1,768,1024]{2,1,0:T(8,128)(2,1)}), bf16[1,768,1024]{2,1,0:T(8,128)(2,1)}) %all-reduce.2.cloned.1.call-update) | async-done | bytes 1572880 | tf_op jit(solution)/shard_map/psum | solution.py:118
  344.7 2.7 copy.122
  (33 shorter events, 0.2 us)
Async XLA Ops:
  7.2 14.0 %copy-start = (bf16[128,1024]{1,0:T(8,128)(2,1)S(1)}, bf16[128,1024]{1,0:T(8,128)(2,1)}, u32[]{:S(2)}) copy-start(bf16[128,1024]{1,0:T(8,128)(2,1)} %param.9) | copy-start | bytes 786436
  7.2 83.9 %all-gather.2.cloned.1.call-start = ((), (), s32[]{:S(2)}) async-start(), calls=%async_computation.6 | async-start | bytes 3342336 | tf_op jit(solution)/shard_map/all_gather | solution.py:80
  10.0 11.0 %copy-start.6 = (s32[128,2]{0,1:T(2,128)}, s32[128,2]{0,1:T(2,128)S(1)}, u32[]{:S(2)}) copy-start(s32[128,2]{0,1:T(2,128)S(1)} %multiply_add_fusion) | copy-start | bytes 3076
  11.6 15.6 %all-to-all-start = ((bf16[32,1,16]{2,1,0:T(2,128)(2,1)}), bf16[32,1,16]{2,1,0:T(2,128)(2,1)S(1)}, u32[]{:S(2)}, u32[]{:S(2)}) async-start(bf16[32,1,16]{2,1,0:T(2,128)(2,1)} %reshape.246), calls=%async_computation | async-start | bytes 32768 | tf_op jit(solution)/shard_map/all_to_all | solution.py:74
  21.1 11.8 %copy-start.9 = (s32[8,1,2]{0,2,1:T(2,128)S(1)}, s32[8,1,2]{0,2,1:T(2,128)}, u32[]{:S(2)}) copy-start(s32[8,1,2]{0,2,1:T(2,128)} %param.15) | copy-start | bytes 196
  21.1 11.8 %copy-start.10 = (f32[16]{0:T(128)S(1)}, f32[16]{0:T(128)}, u32[]{:S(2)}) copy-start(f32[16]{0:T(128)} %param.17) | copy-start | bytes 196
  21.1 12.0 %copy-start.13 = (s32[1,6]{1,0:T(1,128)S(1)}, s32[1,6]{1,0:T(1,128)}, u32[]{:S(2)}) copy-start(s32[1,6]{1,0:T(1,128)} %param.16) | copy-start | bytes 76
  21.2 12.9 %copy-start.4 = (bf16[128,1024]{1,0:T(8,128)(2,1)S(1)}, bf16[128,1024]{1,0:T(8,128)(2,1)}, u32[]{:S(2)}) copy-start(bf16[128,1024]{1,0:T(8,128)(2,1)} %param.10) | copy-start | bytes 786436
  27.2 67.1 %all-to-all-start.2 = ((bf16[32,1,16,1024]{3,2,1,0:T(8,128)(2,1)}), bf16[32,1,16,1024]{3,2,1,0:T(8,128)(2,1)}, u32[]{:S(2)}, u32[]{:S(2)}) async-start(bf16[32,1,16,1024]{3,2,1,0:T(8,128)(2,1)} %bitcast.19), calls=%async_computation.2 | async-start | bytes 2097152 | tf_op jit(solution)/shard_map/all_to_all | solution.py:72
  94.2 23.4 %all-to-all-start.1 = ((bf16[32,1,16,1024]{3,2,1,0:T(8,128)(2,1)}), bf16[32,1,16,1024]{3,2,1,0:T(8,128)(2,1)}, u32[]{:S(2)}, u32[]{:S(2)}) async-start(bf16[32,1,16,1024]{3,2,1,0:T(8,128)(2,1)} %bitcast.139), calls=%async_computation.1 | async-start | bytes 2097152 | tf_op jit(solution)/shard_map/all_to_all | solution.py:73
  101.5 101.0 %reduce-scatter.4.cloned.1.call-start = ((), (), s32[]{:S(2)}) async-start(), calls=%async_computation.8 | async-start | bytes 3342336
  102.5 2.9 copy-start.1
  105.3 1.7 copy-start.2
  107.1 10.6 %copy-start.8 = (f32[768]{0:T(1024)S(1)}, f32[768]{0:T(1024)}, u32[]{:S(2)}) copy-start(f32[768]{0:T(1024)} %broadcast_bitcast_fusion.1) | copy-start | bytes 9220
  107.1 10.6 %copy-start.11 = (bf16[1,768,1024]{2,1,0:T(8,128)(2,1)S(1)}, bf16[1,768,1024]{2,1,0:T(8,128)(2,1)}, u32[]{:S(2)}) copy-start(bf16[1,768,1024]{2,1,0:T(8,128)(2,1)} %param.14) | copy-start | bytes 4718596
  117.6 9.2 %slice-start = ((s8[6291456]{0:T(1024)(128)(4,1)}), s8[4194304]{0:T(1024)(128)(4,1)S(1)}, s32[]{:S(2)}) async-start(s8[6291456]{0:T(1024)(128)(4,1)} %bitcast.136), calls=%async_computation.9 | async-start | bytes 8388608
  122.9 3.8 %copy-start.15 = (bf16[32,16,768]{2,0,1:T(8,128)(2,1)}, bf16[32,16,768]{2,0,1:T(8,128)(2,1)S(1)}, u32[]{:S(2)}) copy-start(bf16[32,16,768]{2,0,1:T(8,128)(2,1)S(1)} %get-tuple-element.24) | copy-start | bytes 2359300
  122.9 3.8 %copy-start.16 = (bf16[32,16,768]{2,0,1:T(8,128)(2,1)}, bf16[32,16,768]{2,0,1:T(8,128)(2,1)S(1)}, u32[]{:S(2)}) copy-start(bf16[32,16,768]{2,0,1:T(8,128)(2,1)S(1)} %get-tuple-element.25) | copy-start | bytes 2359300
  123.0 3.9 %slice-start.1 = ((s8[6291456]{0:T(1024)(128)(4,1)}), s8[2097152]{0:T(1024)(128)(4,1)S(1)}, s32[]{:S(2)}) async-start(s8[6291456]{0:T(1024)(128)(4,1)} %bitcast.136), calls=%async_computation.10 | async-start | bytes 4194304
  131.6 1.4 copy-start.12
  131.6 1.6 copy-start.14
  135.8 22.0 %all-to-all-start.4 = ((bf16[32,1,16,1024]{3,2,1,0:T(8,128)(2,1)}), bf16[32,1,16,1024]{3,2,1,0:T(8,128)(2,1)}, u32[]{:S(2)}, u32[]{:S(2)}) async-start(bf16[32,1,16,1024]{3,2,1,0:T(8,128)(2,1)} %copy.86), calls=%async_computation.4 | async-start | bytes 2097152 | tf_op jit(solution)/shard_map/all_to_all | solution.py:102
  141.6 4.4 %copy-start.3 = (bf16[1024,1536,1]{0,1,2:T(8,128)(2,1)S(1)}, bf16[1024,1536,1]{0,1,2:T(8,128)(2,1)}, u32[]{:S(2)}) copy-start(bf16[1024,1536,1]{0,1,2:T(8,128)(2,1)} %copy-done.2) | copy-start | bytes 9437188
  141.6 203.2 %all-reduce.2.cloned.1.call-start = ((), (), s32[]{:S(2)}) async-start(), calls=%async_computation.7 | async-start | bytes 3145728 | tf_op jit(solution)/shard_map/psum | solution.py:118
  149.1 13.7 %copy-start.5 = (bf16[128,1024]{1,0:T(8,128)(2,1)S(1)}, bf16[128,1024]{1,0:T(8,128)(2,1)}, u32[]{:S(2)}) copy-start(bf16[128,1024]{1,0:T(8,128)(2,1)} %param.10) | copy-start | bytes 786436
  149.1 13.8 %copy-start.7 = (s32[128,2]{0,1:T(2,128)S(1)}, s32[128,2]{0,1:T(2,128)}, u32[]{:S(2)}) copy-start(s32[128,2]{0,1:T(2,128)} %copy-done.6) | copy-start | bytes 3076
  157.8 21.3 %all-to-all-start.3 = ((bf16[32,1,16,1024]{3,2,1,0:T(8,128)(2,1)}), bf16[32,1,16,1024]{3,2,1,0:T(8,128)(2,1)S(1)}, u32[]{:S(2)}, u32[]{:S(2)}) async-start(bf16[32,1,16,1024]{3,2,1,0:T(8,128)(2,1)} %copy.85), calls=%async_computation.3 | async-start | bytes 2097152 | tf_op jit(solution)/shard_map/all_to_all | solution.py:97
Sparse Core Ops, SparseCore 0:
  10.1 80.9 all-gather.1
  131.7 70.7 reduce-scatter.3
  205.4 139.2 all-reduce.1
where the time goes:
time: 355 us; the launch traced here: 354 us
  waiting for transfers between devices  250 us (70%)
  starting transfers between devices  33.6 us (9%)
  matrix products  29.9 us (8%)
  local copies, waits for them, and re-layouts  22.4 us (6%)
  between operations  14.1 us (4%)
  other arithmetic  4.22 us (1%)
    psum x1, waiting for transfers between devices, body(): down_grad = lax.psum(down_part.astype(jnp.bfloat16), 'dp')  140 us
    all_gather x1, waiting for transfers between devices, body(): gathered = lax.all_gather(gate_up_weight, 'dp', axis=0, tiled=True)  55.5 us
    unnamed x4, waiting for transfers between devices  23.1 us
    all_to_all x1, waiting for transfers between devices, body(): lax.all_to_all(row_grads, 'expert', split_axis=0, concat_axis=0, tiled=True)  13.8 us
    unnamed x45, local copies, waits for them, and re-layouts  13.5 us
    all_to_all x1, starting transfers between devices, body(): lax.all_to_all(send_probs, 'expert', split_axis=0, concat_axis=0, tiled=T...  9.4 us
    all_to_all x1, starting transfers between devices, body(): lax.all_to_all(send_grads, 'expert', split_axis=0, concat_axis=0, tiled=T...  7.21 us
    all_to_all x1, waiting for transfers between devices, body(): lax.all_to_all(expert_out.astype(jnp.bfloat16), 'expert', split_axis=0, c...  7.1 us
  transfers between devices with their start and end apart: 8, of which 7 were waited for; matrix products, arithmetic and copies ran while one was open for 10% of the time, Pallas kernels for 0%

commit v1 on v0

--- a/solution.py
+++ b/solution.py
@@ -4,6 +4,11 @@
 from jax.sharding import PartitionSpec as P
 
 QBLOCK = 128
+
+
+def gather_and_add(x, axis):
+    shards = lax.all_gather(x, axis)
+    return jnp.sum(shards, axis=0)
 
 
 def lookup(level_index, level_table):
@@ -115,7 +120,7 @@
         jnp.einsum("sjcf,sjcd->jfd", weighted, recv_grads, preferred_element_type=f32)
         * down_scale[:, :, None]
     )
-    down_grad = lax.psum(down_part.astype(jnp.bfloat16), "dp")
+    down_grad = gather_and_add(down_part.astype(jnp.bfloat16), "dp")
     return (token_grad, prob_grad, gate_up_grad, down_grad)
 
 

time: 355 us -> 501 us (1.41)
  the two profiles are of different devices: /device:TPU:2 before, /device:TPU:1 now
where the time goes in v1:
time: 501 us; the launch traced here: 500 us
  waiting for transfers between devices  377 us (75%)
  starting transfers between devices  40.6 us (8%)
  matrix products  29.6 us (6%)
  other arithmetic  19.1 us (4%)
  local copies, waits for them, and re-layouts  18.7 us (4%)
  between operations  14.1 us (3%)
    all_gather x1, waiting for transfers between devices, gather_and_add(): shards = lax.all_gather(x, axis)  281 us
    all_gather x1, waiting for transfers between devices, body(): gathered = lax.all_gather(gate_up_weight, 'dp', axis=0, tiled=True)  47 us
    all_to_all x1, starting transfers between devices, body(): lax.all_to_all(send_grads, 'expert', split_axis=0, concat_axis=0, tiled=T...  16.3 us
    reduce_sum x1, other arithmetic, gather_and_add(): return jnp.sum(shards, axis=0)  14.9 us
    all_to_all x1, waiting for transfers between devices, body(): lax.all_to_all(row_grads, 'expert', split_axis=0, concat_axis=0, tiled=True)  14.9 us
    all_to_all x1, waiting for transfers between devices, body(): lax.all_to_all(expert_out.astype(jnp.bfloat16), 'expert', split_axis=0, c...  12.5 us
    all_to_all x1, starting transfers between devices, body(): lax.all_to_all(send_probs, 'expert', split_axis=0, concat_axis=0, tiled=T...  10.4 us
    unnamed x40, local copies, waits for them, and re-layouts  10.4 us
  transfers between devices with their start and end apart: 8, of which 7 were waited for; matrix products, arithmetic and copies ran while one was open for 7% of the time, Pallas kernels for 0%

profile of v1, /device:TPU:1, one launch (start us, length us, event | category | flops | bytes accessed | tf_op | source)
XLA Modules:
  0.0 499.6 jit_solution(4482076182277232123)
XLA Ops:
  7.2 0.0 copy-start
  7.2 0.0 all-gather.4.cloned.1.call-start
  7.2 0.7 all-gather.4.cloned.1.call-update
  7.9 0.8 copy.74
  8.7 0.1 eq.95
  8.8 0.2 fusion.15
  9.1 0.1 reduce_sum.53
  9.2 0.1 copy.75
  9.3 0.7 multiply_add_fusion
  10.0 0.9 fusion.33
  10.9 0.7 reshape.250
  11.6 10.4 %all-to-all-start = ((bf16[32,1,16]{2,1,0:T(2,128)(2,1)}), bf16[32,1,16]{2,1,0:T(2,128)(2,1)S(1)}, u32[]{:S(2)}, u32[]{:S(2)}) async-start(bf16[32,1,16]{2,1,0:T(2,128)(2,1)} %reshape.250), calls=%async_computation | async-start | bytes 32768 | tf_op jit(solution)/shard_map/all_to_all | solution.py:79
  22.0 0.1 fusion.34
  22.1 0.0 copy-start.7
  22.1 0.0 copy-start.8
  22.1 0.0 copy-start.11
  22.1 0.0 copy-start.5
  22.2 0.0 copy-done
  22.2 1.4 convolution_convert_fusion.1
  23.6 5.3 %all-to-all-done = bf16[32,1,16]{2,1,0:T(2,128)(2,1)S(1)} async-done(((bf16[32,1,16]{2,1,0:T(2,128)(2,1)}), bf16[32,1,16]{2,1,0:T(2,128)(2,1)S(1)}, u32[]{:S(2)}, u32[]{:S(2)}) %all-to-all-start) | async-done | bytes 1056 | tf_op jit(solution)/shard_map/all_to_all | solution.py:79
  28.9 4.9 all-to-all-start.2
  33.9 0.2 select_reduce_fusion
  34.0 0.1 broadcast_bitcast_fusion
  34.1 0.2 fusion.42
  34.3 0.1 broadcast_bitcast_fusion.1
  34.4 0.0 copy-done.5
  34.4 1.5 convolution_convert_fusion.2
  35.9 0.1 copy.78
  35.9 47.0 %all-gather.4.cloned.1.call-done = bf16[1024,1,1536]{2,0,1:T(8,128)(2,1)} async-done(((bf16[64,1,1536]{2,0,1:T(8,128)(2,1)}), bf16[1024,1,1536]{2,0,1:T(8,128)(2,1)}) %all-gather.4.cloned.1.call-update) | async-done | bytes 3145744 | tf_op jit(solution)/shard_map/all_gather | solution.py:85
  83.0 3.2 copy.76
  86.2 0.0 all-to-all-done.2
  86.2 16.3 %all-to-all-start.1 = ((bf16[32,1,16,1024]{3,2,1,0:T(8,128)(2,1)}), bf16[32,1,16,1024]{3,2,1,0:T(8,128)(2,1)}, u32[]{:S(2)}, u32[]{:S(2)}) async-start(bf16[32,1,16,1024]{3,2,1,0:T(8,128)(2,1)} %bitcast.138), calls=%async_computation.1 | async-start | bytes 2097152 | tf_op jit(solution)/shard_map/all_to_all | solution.py:78
  102.4 0.2 reduce-scatter.4.cloned.1.call-start
  102.7 0.8 broadcast_in_dim.14
  103.5 1.2 fusion.3
  104.7 1.7 copy-done.2
  106.3 1.7 copy-done.3
  108.0 5.1 %convolution_bitcast_fusion = f32[32,1,16,1536]{3,0,2,1:T(8,128)} fusion(bf16[1024,1536,1]{0,1,2:T(8,128)(2,1)S(1)} %fusion.3, bf16[32,1,16,1024]{3,2,1,0:T(8,128)(2,1)} %all-to-all-done.2), kind=kOutput, calls=%fused_computation.4 | convolution fusion | flops 1610612736 | bytes 7340032 | tf_op jit(solution)/shard_map/sjcd,djf->sjcf/dot_general | solution.py:87
  113.2 6.5 %all-to-all-done.1 = bf16[32,1,16,1024]{3,2,1,0:T(8,128)(2,1)} async-done(((bf16[32,1,16,1024]{3,2,1,0:T(8,128)(2,1)}), bf16[32,1,16,1024]{3,2,1,0:T(8,128)(2,1)}, u32[]{:S(2)}, u32[]{:S(2)}) %all-to-all-start.1) | async-done | bytes 1048608 | tf_op jit(solution)/shard_map/all_to_all | solution.py:78
  119.7 5.3 %fusion.30 = (bf16[32,16,768]{2,0,1:T(8,128)(2,1)S(1)}, bf16[32,16,768]{2,0,1:T(8,128)(2,1)S(1)}, bf16[32,1,16,768]{3,0,2,1:T(8,128)(2,1)}) fusion(f32[32,1,16,1536]{3,0,2,1:T(8,128)} %convolution_bitcast_fusion, bf16[32,1,16,1024]{3,2,1,0:T(8,128)(2,1)} %all-to-all-done.1, bf16[1,768,1024]{2,1,0:T(8,128)(2,1)S(1)} %copy-done.9, ...), kind=kOutput, calls=%fused_computation.48 | convolution fusion | flops 813957120 | bytes 8131584 | tf_op jit(solution)/shard_map/sjcd,jfd->sjcf/dot_general | solution.py:93
  125.0 3.8 fusion.16
  128.8 1.8 fusion.2
  130.6 3.0 copy.96
  133.6 0.0 reduce-scatter.4.cloned.1.call-update
  133.6 0.0 all-gather.6.cloned.1.call-start
  133.7 1.1 copy-done.12
  134.7 3.7 fusion.4
  138.4 0.0 all-gather.6.cloned.1.call-update
  138.5 1.1 fusion.11
  139.6 1.6 copy.86
  141.1 4.9 all-to-all-start.4
  146.0 3.2 fusion.12
  149.2 0.0 copy-start.6
  149.2 1.6 copy.85
  150.8 12.5 %all-to-all-done.4 = bf16[32,1,16,1024]{3,2,1,0:T(8,128)(2,1)} async-done(((bf16[32,1,16,1024]{3,2,1,0:T(8,128)(2,1)}), bf16[32,1,16,1024]{3,2,1,0:T(8,128)(2,1)}, u32[]{:S(2)}, u32[]{:S(2)}) %all-to-all-start.4) | async-done | bytes 1048608 | tf_op jit(solution)/shard_map/all_to_all | solution.py:107
  163.3 4.0 all-to-all-start.3
  167.4 2.4 fusion.13
  169.7 14.9 %all-to-all-done.3 = bf16[32,1,16,1024]{3,2,1,0:T(8,128)(2,1)S(1)} async-done(((bf16[32,1,16,1024]{3,2,1,0:T(8,128)(2,1)}), bf16[32,1,16,1024]{3,2,1,0:T(8,128)(2,1)S(1)}, u32[]{:S(2)}, u32[]{:S(2)}) %all-to-all-start.3) | async-done | bytes 1048608 | tf_op jit(solution)/shard_map/all_to_all | solution.py:102
  184.6 1.0 convolution_convert_fusion.4
  185.6 9.6 %reduce-scatter.4.cloned.1.call-done = bf16[64,1536]{1,0:T(8,128)(2,1)} async-done(((bf16[1024,1536]{1,0:T(8,128)(2,1)}), bf16[64,1536]{1,0:T(8,128)(2,1)}) %reduce-scatter.4.cloned.1.call-update) | async-done | bytes 196624
  195.2 1.1 copy.97
  196.3 0.8 copy.88
  197.2 280.9 %all-gather.6.cloned.1.call-done = bf16[12288,1024]{1,0:T(8,128)(2,1)} async-done(((bf16[768,1024]{1,0:T(8,128)(2,1)}), bf16[12288,1024]{1,0:T(8,128)(2,1)}) %all-gather.6.cloned.1.call-update) | async-done | bytes 25165840 | tf_op jit(solution)/shard_map/all_gather | solution.py:10
  478.1 14.9 %reduce.4 = bf16[768,1024]{1,0:T(8,128)(2,1)} reduce(bf16[16,768,1024]{2,1,0:T(8,128)(2,1)} %bitcast.137, bf16[]{:T(256)} %constant.12.clone.1), dimensions={0}, to_apply=%region_5.0 | reduce | flops 11796480 | bytes 26738690 | tf_op jit(solution)/shard_map/reduce_sum | solution.py:11
  (29 shorter events, 0.2 us)
Async XLA Ops:
  7.2 15.0 %copy-start = (bf16[128,1024]{1,0:T(8,128)(2,1)S(1)}, bf16[128,1024]{1,0:T(8,128)(2,1)}, u32[]{:S(2)}) copy-start(bf16[128,1024]{1,0:T(8,128)(2,1)} %param.9) | copy-start | bytes 786436
  7.2 75.8 %all-gather.4.cloned.1.call-start = ((), (), s32[]{:S(2)}) async-start(), calls=%async_computation.6 | async-start | bytes 3342336 | tf_op jit(solution)/shard_map/all_gather | solution.py:85
  11.6 17.3 %all-to-all-start = ((bf16[32,1,16]{2,1,0:T(2,128)(2,1)}), bf16[32,1,16]{2,1,0:T(2,128)(2,1)S(1)}, u32[]{:S(2)}, u32[]{:S(2)}) async-start(bf16[32,1,16]{2,1,0:T(2,128)(2,1)} %reshape.250), calls=%async_computation | async-start | bytes 32768 | tf_op jit(solution)/shard_map/all_to_all | solution.py:79
  22.1 11.8 %copy-start.7 = (s32[8,1,2]{0,2,1:T(2,128)S(1)}, s32[8,1,2]{0,2,1:T(2,128)}, u32[]{:S(2)}) copy-start(s32[8,1,2]{0,2,1:T(2,128)} %param.15) | copy-start | bytes 196
  22.1 11.8 %copy-start.8 = (f32[16]{0:T(128)S(1)}, f32[16]{0:T(128)}, u32[]{:S(2)}) copy-start(f32[16]{0:T(128)} %param.17) | copy-start | bytes 196
  22.1 12.0 %copy-start.11 = (s32[1,6]{1,0:T(1,128)S(1)}, s32[1,6]{1,0:T(1,128)}, u32[]{:S(2)}) copy-start(s32[1,6]{1,0:T(1,128)} %param.16) | copy-start | bytes 76
  22.1 12.3 %copy-start.5 = (bf16[128,1024]{1,0:T(8,128)(2,1)S(1)}, bf16[128,1024]{1,0:T(8,128)(2,1)}, u32[]{:S(2)}) copy-start(bf16[128,1024]{1,0:T(8,128)(2,1)} %param.10) | copy-start | bytes 786436
  28.9 57.2 %all-to-all-start.2 = ((bf16[32,1,16,1024]{3,2,1,0:T(8,128)(2,1)}), bf16[32,1,16,1024]{3,2,1,0:T(8,128)(2,1)}, u32[]{:S(2)}, u32[]{:S(2)}) async-start(bf16[32,1,16,1024]{3,2,1,0:T(8,128)(2,1)} %bitcast.19), calls=%async_computation.2 | async-start | bytes 2097152 | tf_op jit(solution)/shard_map/all_to_all | solution.py:77
  86.2 33.5 %all-to-all-start.1 = ((bf16[32,1,16,1024]{3,2,1,0:T(8,128)(2,1)}), bf16[32,1,16,1024]{3,2,1,0:T(8,128)(2,1)}, u32[]{:S(2)}, u32[]{:S(2)}) async-start(bf16[32,1,16,1024]{3,2,1,0:T(8,128)(2,1)} %bitcast.138), calls=%async_computation.1 | async-start | bytes 2097152 | tf_op jit(solution)/shard_map/all_to_all | solution.py:78
  102.4 92.8 %reduce-scatter.4.cloned.1.call-start = ((), (), s32[]{:S(2)}) async-start(), calls=%async_computation.8 | async-start | bytes 3342336
  103.4 2.9 copy-start.2
  106.3 1.7 copy-start.3
  108.0 11.6 %copy-start.9 = (bf16[1,768,1024]{2,1,0:T(8,128)(2,1)S(1)}, bf16[1,768,1024]{2,1,0:T(8,128)(2,1)}, u32[]{:S(2)}) copy-start(bf16[1,768,1024]{2,1,0:T(8,128)(2,1)} %param.14) | copy-start | bytes 4718596
  119.7 9.2 %slice-start = ((s8[6291456]{0:T(1024)(128)(4,1)}), s8[4194304]{0:T(1024)(128)(4,1)S(1)}, s32[]{:S(2)}) async-start(s8[6291456]{0:T(1024)(128)(4,1)} %bitcast.134), calls=%async_computation.9 | async-start | bytes 8388608
  124.9 3.8 copy-start.13
  124.9 3.8 copy-start.14
  124.9 3.9 slice-start.1
  133.6 1.1 copy-start.12
  133.6 344.5 %all-gather.6.cloned.1.call-start = ((), (), s32[]{:S(2)}) async-start(), calls=%async_computation.7 | async-start | bytes 26738688 | tf_op jit(solution)/shard_map/all_gather | solution.py:10
  134.7 3.7 copy-start.10
  139.6 6.4 %copy-start.4 = (bf16[1024,1536,1]{0,1,2:T(8,128)(2,1)S(1)}, bf16[1024,1536,1]{0,1,2:T(8,128)(2,1)}, u32[]{:S(2)}) copy-start(bf16[1024,1536,1]{0,1,2:T(8,128)(2,1)} %copy-done.3) | copy-start | bytes 9437188
  141.1 22.2 %all-to-all-start.4 = ((bf16[32,1,16,1024]{3,2,1,0:T(8,128)(2,1)}), bf16[32,1,16,1024]{3,2,1,0:T(8,128)(2,1)}, u32[]{:S(2)}, u32[]{:S(2)}) async-start(bf16[32,1,16,1024]{3,2,1,0:T(8,128)(2,1)} %copy.86), calls=%async_computation.4 | async-start | bytes 2097152 | tf_op jit(solution)/shard_map/all_to_all | solution.py:107
  149.2 18.1 %copy-start.6 = (bf16[128,1024]{1,0:T(8,128)(2,1)S(1)}, bf16[128,1024]{1,0:T(8,128)(2,1)}, u32[]{:S(2)}) copy-start(bf16[128,1024]{1,0:T(8,128)(2,1)} %param.10) | copy-start | bytes 786436
  163.3 21.3 %all-to-all-start.3 = ((bf16[32,1,16,1024]{3,2,1,0:T(8,128)(2,1)}), bf16[32,1,16,1024]{3,2,1,0:T(8,128)(2,1)S(1)}, u32[]{:S(2)}, u32[]{:S(2)}) async-start(bf16[32,1,16,1024]{3,2,1,0:T(8,128)(2,1)} %copy.85), calls=%async_computation.3 | async-start | bytes 2097152 | tf_op jit(solution)/shard_map/all_to_all | solution.py:102
  478.1 14.9 %copy-start.1 = (bf16[128,1024]{1,0:T(8,128)(2,1)S(1)}, bf16[128,1024]{1,0:T(8,128)(2,1)}, u32[]{:S(2)}) copy-start(bf16[128,1024]{1,0:T(8,128)(2,1)} %param.9) | copy-start | bytes 786436
Sparse Core Ops, SparseCore 0:
  10.1 72.8 all-gather.3
  133.8 61.3 reduce-scatter.3
  197.8 280.2 all-gather.5
